TPU v7x, 256 devices: a whole 4x4x8 slice. The times are simulated.
256 devices in a mesh: seq: 32 (over x, z_hi, core), batch: 8 (over z_lo, y).
Axes of the slice: x: 4, y: 4, z: 8 (z_hi: 4, z_lo: 2; z = z_hi * 2 + z_lo), core: 2. Of those that a mesh axis runs over, the one named last changes fastest.
Arguments:
- activations: bfloat16 [8, 16384, 1536], P('batch', 'seq'), may hold values from -60 to 60
- cotangent: bfloat16 [8, 16384, 1536], P('batch', 'seq'), may hold values from -6 to 6
- contig_lengths: int32 [8, 4], P('batch'), may hold values from 1 to 8192, 16384 in all within a row
- gain_input: float32 [1536], replicated, may hold values from 0.1 to 1.9
- tap_weights: bfloat16 [3, 1536, 768], replicated, may hold values from -0.09375 to 0.09375
- gain_middle: float32 [768], replicated, may hold values from 0.1 to 1.9
- point_weights: bfloat16 [768, 1536], replicated, may hold values from -0.21875 to 0.21875
Outputs:
- block_output: bfloat16 [8, 16384, 1536], P('batch', 'seq')
- input_grad: bfloat16 [8, 16384, 1536], P('batch', 'seq')
- gain_input_grad: float32 [1536], replicated
- gain_middle_grad: float32 [768], replicated
Inputs may be any that keep to these rules, and one draw needn't show every extreme that they name: `contig_lengths`: row w lists in order the lengths of the 4 contigs packed into window w; they sum to 16384.
All inputs are finite; a program needn't handle non-finite values.
Results may differ from a plain program's by a relative error of at most 0.0065.
Values may be sent and summed in bfloat16 or wider, within the bound.
A program may use at most 64 MiB of HBM per device.

v0:
```python
import math

import jax
import jax.numpy as jnp
from jax import lax
from jax.sharding import PartitionSpec as P

SPAN = 2


epsilon = 1e-06


def shifted(x, axis, by):
    peers = lax.axis_size(axis)
    pairs = [(i, i + by) for i in range(peers) if 0 <= i + by < peers]
    return lax.ppermute(x, axis, pairs)


def norm_activate(values, scales):
    mean_square = jnp.mean(values * values, axis=-1, keepdims=True)
    return jax.nn.gelu(values * lax.rsqrt(mean_square + epsilon) * scales, approximate=True)


def contig_owner(lengths, positions):
    bounds = jnp.cumsum(lengths)
    return jnp.sum((positions[:, None] >= bounds[None, :]).astype(jnp.int32), axis=1)


def body(
    activations, cotangent, contig_lengths, gain_input, tap_weights, gain_middle, point_weights
):
    signal = activations[0]
    upstream = cotangent[0]
    lengths = contig_lengths[0]
    shard_rows = signal.shape[0]
    seq_count = lax.axis_size("seq")
    tap_reach = SPAN * shard_rows
    total_length = shard_rows * seq_count
    positions = lax.axis_index("seq") * shard_rows + jnp.arange(shard_rows, dtype=jnp.int32)
    owners = contig_owner(lengths, positions)
    before_valid = (
        (positions >= tap_reach) & (contig_owner(lengths, positions - tap_reach) == owners)
    ).astype(jnp.float32)[:, None]
    after_valid = (
        (positions < total_length - tap_reach)
        & (contig_owner(lengths, positions + tap_reach) == owners)
    ).astype(jnp.float32)[:, None]
    tap_before = tap_weights[0]
    tap_center = tap_weights[1]
    tap_after = tap_weights[2]
    normed, input_vjp = jax.vjp(norm_activate, signal.astype(jnp.float32), gain_input)
    hidden = normed.astype(jnp.bfloat16)
    hidden_before = shifted(hidden, "seq", SPAN)
    hidden_after = shifted(hidden, "seq", -SPAN)
    combined = jnp.dot(hidden, tap_center, preferred_element_type=jnp.float32)
    combined = combined + before_valid * jnp.dot(
        hidden_before, tap_before, preferred_element_type=jnp.float32
    )
    combined = combined + after_valid * jnp.dot(
        hidden_after, tap_after, preferred_element_type=jnp.float32
    )
    middle_f, middle_vjp = jax.vjp(norm_activate, combined, gain_middle)
    middle = middle_f.astype(jnp.bfloat16)
    output = (
        signal.astype(jnp.float32)
        + jnp.dot(middle, point_weights, preferred_element_type=jnp.float32)
    ).astype(jnp.bfloat16)
    grad_middle = jnp.dot(upstream, point_weights.T, preferred_element_type=jnp.float32)
    grad_combined_f, middle_terms = middle_vjp(grad_middle)
    grad_combined = grad_combined_f.astype(jnp.bfloat16)
    grad_hidden = jnp.dot(grad_combined, tap_center.T, preferred_element_type=jnp.float32)
    forward_terms = jnp.dot(grad_combined, tap_after.T, preferred_element_type=jnp.float32)
    backward_terms = jnp.dot(grad_combined, tap_before.T, preferred_element_type=jnp.float32)
    terms_before = shifted(forward_terms.astype(jnp.bfloat16), "seq", SPAN).astype(
        forward_terms.dtype
    )
    terms_after = shifted(backward_terms.astype(jnp.bfloat16), "seq", -SPAN).astype(
        backward_terms.dtype
    )
    grad_hidden = grad_hidden + before_valid * terms_before + after_valid * terms_after
    grad_signal, input_terms = input_vjp(grad_hidden)
    grad_output = (upstream.astype(jnp.float32) + grad_signal).astype(jnp.bfloat16)
    summed = lax.psum((input_terms, middle_terms), ("seq", "batch"))
    factor = 1.0 / math.sqrt(lax.axis_size("batch") * seq_count * shard_rows)
    return (output[None], grad_output[None], summed[0] * factor, summed[1] * factor)


def solution(mesh):
    placed = (
        P("batch", "seq", None),
        P("batch", "seq", None),
        P("batch", None),
        P(),
        P(),
        P(),
        P(),
    )
    return jax.shard_map(
        body,
        mesh=mesh,
        in_specs=placed,
        out_specs=(P("batch", "seq", None), P("batch", "seq", None), P(), P()),
        check_vma=False,
    )
```

profile of v0, /device:TPU:1, one launch (start us, length us, event | category | flops | bytes accessed | tf_op | source)
XLA Modules:
  0.0 262.9 jit_solution(1992387566974360325)
XLA Ops:
  0.6 0.0 copy-start
  0.6 0.0 copy-start.1
  0.7 0.0 copy-start.4
  0.7 1.9 fusion.16
  2.6 0.1 copy-done.1
  2.7 3.2 %fusion.12 = bf16[512,1536]{1,0:T(8,128)(2,1)} fusion(bf16[1,512,1536]{2,1,0:T(8,128)(2,1)S(1)} %copy-done.1, f32[1536]{0:T(1024)} %param.10, f32[512]{0:T(512)S(1)} %fusion.88), kind=kLoop, calls=%fused_computation.18 | loop fusion | flops 9437184 | bytes 3153920 | tf_op jit(solution)/shard_map/convert_element_type | solution.py:53
  5.9 6.9 %collective-permute-start = (bf16[512,1536]{1,0:T(8,128)(2,1)}, bf16[512,1536]{1,0:T(8,128)(2,1)}, u32[]{:S(2)}, u32[]{:S(2)}) collective-permute-start(bf16[512,1536]{1,0:T(8,128)(2,1)} %fusion.12), channel_id=1, source_target_pairs={{0,16},{8,24},{16,32},{24,40},{32,48},{40,56},{48,64},{56,72},{64,... | collective-permute-start | bytes 4718600 | tf_op jit(solution)/shard_map/ppermute | solution.py:17
  12.8 1.3 collective-permute-start.1
  14.1 0.2 reduce-window.8
  14.3 0.1 convert_reduce_fusion.2
  14.4 4.4 %fusion.42 = f32[512,768]{1,0:T(8,128)S(1)} fusion(bf16[3,1536,768]{2,1,0:T(8,128)(2,1)} %param.11, bf16[1,512,1536]{2,1,0:T(8,128)(2,1)} %param.7, f32[1536]{0:T(1024)S(1)} %copy-done.4, f32[512]{0:T(512)S(1)} %fusion.88), kind=kOutput, calls=%fused_computation.51 | convolution fusion | flops 1217396736 | bytes 5513216 | tf_op jit(solution)/shard_map/dot_general | solution.py:56
  18.8 38.5 %collective-permute-done = bf16[512,1536]{1,0:T(8,128)(2,1)} collective-permute-done((bf16[512,1536]{1,0:T(8,128)(2,1)}, bf16[512,1536]{1,0:T(8,128)(2,1)}, u32[]{:S(2)}, u32[]{:S(2)}) %collective-permute-start) | collective-permute-done | bytes 1572896 | tf_op jit(solution)/shard_map/ppermute | solution.py:17
  57.3 3.5 %fusion.38 = f32[512,768]{1,0:T(8,128)S(1)} fusion(bf16[512,1536]{1,0:T(8,128)(2,1)} %collective-permute-done, bf16[3,1536,768]{2,1,0:T(8,128)(2,1)} %param.11), kind=kOutput, calls=%fused_computation.47 | convolution fusion | flops 1207959552 | bytes 5505024 | tf_op jit(solution)/shard_map/dot_general | solution.py:57
  60.9 25.1 %collective-permute-done.1 = bf16[512,1536]{1,0:T(8,128)(2,1)} collective-permute-done((bf16[512,1536]{1,0:T(8,128)(2,1)}, bf16[512,1536]{1,0:T(8,128)(2,1)}, u32[]{:S(2)}, u32[]{:S(2)}) %collective-permute-start.1) | collective-permute-done | bytes 1572896 | tf_op jit(solution)/shard_map/ppermute | solution.py:17
  86.0 3.8 %multiply_reduce_fusion.2 = (f32[512]{0:T(512)S(1)}, f32[512,768]{1,0:T(8,128)S(1)}) fusion(bf16[512,1536]{1,0:T(8,128)(2,1)} %collective-permute-done.1, bf16[3,1536,768]{2,1,0:T(8,128)(2,1)} %param.11, f32[512]{0:T(512)S(1)} %get-tuple-element.14, f32[512,768]{1,0:T(8,128)S(1)} %fusion.42, f32[512,768]{1,0:T(8,128)S(1)} %fusion.38, ...), kind=kOutput, calls=%fused_computation.75 | convolution fusion | flops 1210318336 | bytes 8656896 | tf_op jit(solution)/shard_map/dot_general | solution.py:60
  89.8 0.0 slice-start
  89.9 2.5 multiply_reduce_fusion
  92.4 0.4 fusion.58
  92.8 0.1 slice-done.1
  92.9 1.4 convolution_convert_fusion
  94.3 0.0 copy-start.2
  94.4 1.4 convolution_convert_fusion.1
  95.8 5.6 %collective-permute-start.2 = (bf16[512,1536]{1,0:T(8,128)(2,1)S(1)}, bf16[512,1536]{1,0:T(8,128)(2,1)S(1)}, u32[]{:S(2)}, u32[]{:S(2)}) collective-permute-start(bf16[512,1536]{1,0:T(8,128)(2,1)S(1)} %convolution_convert_fusion.1), channel_id=1, source_target_pairs={{0,16},{8,24},{16,32},{24,40},{32,48},{40,56},{48,64},{56,72},{64,... | collective-permute-start | bytes 4718600 | tf_op jit(solution)/shard_map/ppermute | solution.py:17
  101.4 1.5 collective-permute-start.3
  102.8 2.8 %fusion.33 = bf16[1,512,1536]{2,1,0:T(8,128)(2,1)} fusion(bf16[768,1536]{1,0:T(8,128)(2,1)S(1)} %copy-done, bf16[1,512,1536]{2,1,0:T(8,128)(2,1)S(1)} %copy-done.2, f32[512,768]{1,0:T(8,128)S(1)} %get-tuple-element.16, f32[768]{0:T(1024)S(1)} %copy-done.5, f32[512]{0:T(512)S(1)} %fusion.89), kind=kOutput, calls=%fused_computation.41 | convolution fusion | flops 1214644224 | bytes 7083008 | tf_op jit(solution)/shard_map/dot_general | solution.py:67
  105.7 62.0 %collective-permute-done.2 = bf16[512,1536]{1,0:T(8,128)(2,1)S(1)} collective-permute-done((bf16[512,1536]{1,0:T(8,128)(2,1)S(1)}, bf16[512,1536]{1,0:T(8,128)(2,1)S(1)}, u32[]{:S(2)}, u32[]{:S(2)}) %collective-permute-start.2) | collective-permute-done | bytes 1572896 | tf_op jit(solution)/shard_map/ppermute | solution.py:17
  167.7 4.3 %collective-permute-done.3 = bf16[512,1536]{1,0:T(8,128)(2,1)S(1)} collective-permute-done((bf16[512,1536]{1,0:T(8,128)(2,1)S(1)}, bf16[512,1536]{1,0:T(8,128)(2,1)S(1)}, u32[]{:S(2)}, u32[]{:S(2)}) %collective-permute-start.3) | collective-permute-done | bytes 1572896 | tf_op jit(solution)/shard_map/ppermute | solution.py:17
  172.0 6.1 %fusion.15 = (f32[1536]{0:T(1024)S(1)}, f32[512]{0:T(512)S(1)}, f32[512,1536]{1,0:T(8,128)}) fusion(bf16[1,512,1536]{2,1,0:T(8,128)(2,1)S(1)} %copy-done.2, f32[512]{0:T(512)S(1)} %fusion.88, f32[1536]{0:T(1024)S(1)} %copy-done.4, bf16[512,1536]{1,0:T(8,128)(2,1)S(1)} %collective-permute-done.3, f32[512]{0:T(512)S(1)} %get-tuple-element.14, ...), kind=kOutput, calls=%fused_computation.21 | convolution fusion | flops 1233909760 | bytes 11032576 | tf_op jit(solution)/shard_map/dot_general | solution.py:72
  178.1 78.7 %all-reduce = (f32[1536]{0:T(1024)S(1)}, f32[768]{0:T(1024)S(1)}) all-reduce(f32[1536]{0:T(1024)S(1)} %get-tuple-element.4, f32[768]{0:T(1024)S(1)} %get-tuple-element.6), channel_id=1, replica_groups=mesh['seq'=32,'batch'=8] {'seq','batch'}, use_global_device_ids=true, to_apply=%region_9.10 | all-reduce | flops 2304 | bytes 18432 | tf_op jit(solution)/shard_map/psum | solution.py:84
  256.8 0.6 broadcast_multiply_fusion
  257.4 0.6 broadcast_multiply_fusion.1
  258.0 4.9 %fusion.59 = bf16[1,512,1536]{2,1,0:T(8,128)(2,1)} fusion(bf16[1,512,1536]{2,1,0:T(8,128)(2,1)} %param.7, f32[512,1536]{1,0:T(8,128)} %get-tuple-element.18, bf16[1,512,1536]{2,1,0:T(8,128)(2,1)} %param.8, f32[512]{0:T(512)S(1)} %multiply_multiply_fusion.6, f32[1536]{0:T(1024)S(1)} %copy-done.4, f32[512]{0:T(512)S(1)} %fusion.88), kind=kLoop, calls=%fused_computation.68 | loop fusion | flops 7077888 | bytes 7874560 | tf_op jit(solution)/shard_map/broadcast_in_dim | solution.py:86
  (19 shorter events, 0.1 us)
Async XLA Ops:
  0.6 89.2 %copy-start = (bf16[768,1536]{1,0:T(8,128)(2,1)S(1)}, bf16[768,1536]{1,0:T(8,128)(2,1)}, u32[]{:S(2)}) copy-start(bf16[768,1536]{1,0:T(8,128)(2,1)} %param.13) | copy-start | bytes 7077892
  0.6 2.0 copy-start.1
  0.7 13.7 %copy-start.4 = (f32[1536]{0:T(1024)S(1)}, f32[1536]{0:T(1024)}, u32[]{:S(2)}) copy-start(f32[1536]{0:T(1024)} %param.10) | copy-start | bytes 18436
  0.7 13.4 %copy-start.6 = (s32[1,4]{1,0:T(1,128)S(1)}, s32[1,4]{1,0:T(1,128)}, u32[]{:S(2)}) copy-start(s32[1,4]{1,0:T(1,128)} %param.9) | copy-start | bytes 52
  5.9 51.4 %collective-permute-start = (bf16[512,1536]{1,0:T(8,128)(2,1)}, bf16[512,1536]{1,0:T(8,128)(2,1)}, u32[]{:S(2)}, u32[]{:S(2)}) collective-permute-start(bf16[512,1536]{1,0:T(8,128)(2,1)} %fusion.12), channel_id=1, source_target_pairs={{0,16},{8,24},{16,32},{24,40},{32,48},{40,56},{48,64},{56,72},{64,... | collective-permute-start | bytes 4718600 | tf_op jit(solution)/shard_map/ppermute | solution.py:17
  12.8 73.2 %collective-permute-start.1 = (bf16[512,1536]{1,0:T(8,128)(2,1)}, bf16[512,1536]{1,0:T(8,128)(2,1)}, u32[]{:S(2)}, u32[]{:S(2)}) collective-permute-start(bf16[512,1536]{1,0:T(8,128)(2,1)} %fusion.12), channel_id=1, source_target_pairs={{16,0},{24,8},{32,16},{40,24},{48,32},{56,40},{64,48},{72,56},{80,... | collective-permute-start | bytes 4718600 | tf_op jit(solution)/shard_map/ppermute | solution.py:17
  86.0 3.9 %copy-start.3 = (bf16[1,512,1536]{2,1,0:T(8,128)(2,1)S(1)}, bf16[1,512,1536]{2,1,0:T(8,128)(2,1)}, u32[]{:S(2)}) copy-start(bf16[1,512,1536]{2,1,0:T(8,128)(2,1)} %param.8) | copy-start | bytes 4718596
  86.0 3.9 %copy-start.5 = (f32[768]{0:T(1024)S(1)}, f32[768]{0:T(1024)}, u32[]{:S(2)}) copy-start(f32[768]{0:T(1024)} %param.12) | copy-start | bytes 9220
  89.8 3.0 %slice-start = ((s8[7077888]{0:T(1024)(128)(4,1)}), s8[4194304]{0:T(1024)(128)(4,1)S(1)}, s32[]{:S(2)}) async-start(s8[7077888]{0:T(1024)(128)(4,1)} %bitcast.116), calls=%async_computation | async-start | bytes 8388608
  89.9 3.1 %slice-start.1 = ((s8[7077888]{0:T(1024)(128)(4,1)}), s8[2883584]{0:T(1024)(128)(4,1)S(1)}, s32[]{:S(2)}) async-start(s8[7077888]{0:T(1024)(128)(4,1)} %bitcast.116), calls=%async_computation.1 | async-start | bytes 5767168
  94.3 8.5 %copy-start.2 = (bf16[1,512,1536]{2,1,0:T(8,128)(2,1)S(1)}, bf16[1,512,1536]{2,1,0:T(8,128)(2,1)}, u32[]{:S(2)}) copy-start(bf16[1,512,1536]{2,1,0:T(8,128)(2,1)} %param.7) | copy-start | bytes 4718596
  95.8 71.9 %collective-permute-start.2 = (bf16[512,1536]{1,0:T(8,128)(2,1)S(1)}, bf16[512,1536]{1,0:T(8,128)(2,1)S(1)}, u32[]{:S(2)}, u32[]{:S(2)}) collective-permute-start(bf16[512,1536]{1,0:T(8,128)(2,1)S(1)} %convolution_convert_fusion.1), channel_id=1, source_target_pairs={{0,16},{8,24},{16,32},{24,40},{32,48},{40,56},{48,64},{56,72},{64,... | collective-permute-start | bytes 4718600 | tf_op jit(solution)/shard_map/ppermute | solution.py:17
  101.4 70.6 %collective-permute-start.3 = (bf16[512,1536]{1,0:T(8,128)(2,1)S(1)}, bf16[512,1536]{1,0:T(8,128)(2,1)S(1)}, u32[]{:S(2)}, u32[]{:S(2)}) collective-permute-start(bf16[512,1536]{1,0:T(8,128)(2,1)S(1)} %convolution_convert_fusion), channel_id=1, source_target_pairs={{16,0},{24,8},{32,16},{40,24},{48,32},{56,40},{64,48},{72,56},{80,... | collective-permute-start | bytes 4718600 | tf_op jit(solution)/shard_map/ppermute | solution.py:17
where the time goes:
time: 263 us
  waiting for transfers between devices  130 us (49%)
  blocking collectives  78.7 us (30%)
  matrix products  26.1 us (10%)
  starting transfers between devices  15.2 us (6%)
  other arithmetic  11.9 us (5%)
    ppermute x4, waiting for transfers between devices, shifted(): return lax.ppermute(x, axis, pairs)  130 us
    psum x1, blocking collectives, body(): summed = lax.psum((input_terms, middle_terms), ('seq', 'batch'))  78.7 us
    ppermute x4, starting transfers between devices, shifted(): return lax.ppermute(x, axis, pairs)  15.2 us
    dot_general x1, matrix products, body(): jnp.dot(grad_combined, tap_center.T, preferred_element_type=jnp.float32)  6.11 us
  transfers between devices with their start and end apart: 4, of which 4 were waited for; matrix products, arithmetic and copies ran while one was open for 4% of the time, Pallas kernels for 0%

commit v1 on v0

v1 whole, which is shorter than its diff:
```python
import functools
import math

import jax
import jax.numpy as jnp
from jax import lax
from jax.experimental import pallas as pl
from jax.experimental.pallas import tpu as pltpu
from jax.sharding import PartitionSpec as P

SPAN = 2
CORES = 2
EPS = 1e-06
ROOT = math.sqrt(2.0 / math.pi)
CUBIC = 0.044715
CHUNK = 128
SUB = 16
MESH = pl.DeviceIdType.MESH
F32 = jnp.float32
BF16 = jnp.bfloat16


def tanh_part(u):
    u2 = u * u
    return u2, jnp.tanh(ROOT * u * (1.0 + CUBIC * u2))


def slope(u, u2, t):
    return 0.5 * (1.0 + t) + 0.5 * u * (1.0 - t * t) * (ROOT * (1.0 + 3.0 * CUBIC * u2))


def nt_dot(a, b):
    return lax.dot_general(a, b, (((1,), (1,)), ((), ())), preferred_element_type=F32)


def nn_dot(a, b):
    return jnp.dot(a, b, preferred_element_type=F32)


def kernel(
    n_seq, n_batch,
    lengths_hbm, act_hbm, ct_hbm, gain_in_hbm, tap_hbm, gain_mid_hbm, point_hbm,
    out_hbm, ing_hbm, gsum_in, gsum_mid,
    lengths, act, ct, gain_in, tap, gain_mid, point,
    hid, send_p, recv_p, cen, gmid, gc, recv_g, mid, gh, out, ing,
    acc_in, acc_mid, slots1, slots2,
    in_sem, act_sem, out_sem, ing_sem,
    p_send, p_recv, g_send, g_recv, r1_send, r1_recv, r2_send, r2_recv,
):
    rows, c = act.shape
    f = mid.shape[1]
    n = rows // CHUNK
    reach = SPAN * rows
    total = rows * n_seq
    seq = lax.axis_index("seq")
    batch = lax.axis_index("batch")
    core = lax.rem(seq, CORES)
    place = seq // CORES
    n_place = n_seq // CORES
    me1 = core * n_batch + batch
    n1 = CORES * n_batch

    def peer1(k):
        j = lax.rem(me1 + k, n1)
        return j, {"seq": seq - core + j // n_batch, "batch": lax.rem(j, n_batch)}

    def peer2(k):
        j = lax.rem(place + k, n_place)
        return j, {"seq": j * CORES + core, "batch": batch}

    barrier = pltpu.get_barrier_semaphore()
    for k in range(1, n_place):
        pl.semaphore_signal(barrier, inc=1, device_id=peer2(k)[1], device_id_type=MESH)
    for k in range(1, n1):
        pl.semaphore_signal(barrier, inc=1, device_id=peer1(k)[1], device_id_type=MESH)

    def part(i):
        return pl.ds(pl.multiple_of(i * CHUNK, CHUNK), CHUNK)

    def load_act(i):
        return pltpu.make_async_copy(act_hbm.at[0, part(i)], act.at[part(i)], act_sem.at[i])

    loads = [
        pltpu.make_async_copy(lengths_hbm, lengths, in_sem.at[0]),
        pltpu.make_async_copy(gain_in_hbm, gain_in, in_sem.at[1]),
        pltpu.make_async_copy(tap_hbm.at[0], tap.at[0], in_sem.at[2]),
        pltpu.make_async_copy(tap_hbm.at[2], tap.at[2], in_sem.at[3]),
        pltpu.make_async_copy(tap_hbm.at[1], tap.at[1], in_sem.at[4]),
        pltpu.make_async_copy(gain_mid_hbm, gain_mid, in_sem.at[5]),
        pltpu.make_async_copy(point_hbm, point, in_sem.at[6]),
        pltpu.make_async_copy(ct_hbm.at[0], ct, in_sem.at[7]),
    ]
    load_act(0).start()
    for k in (1, 2, 3):
        loads[k].start()
    for i in range(1, n):
        load_act(i).start()
    for k in (0, 4, 5, 6, 7):
        loads[k].start()

    ahead = {"seq": peer2(1)[1]["seq"]}
    behind = {"seq": peer2(n_place - 1)[1]["seq"]}

    def push(src, dst, send, recv, way, i):
        return pltpu.make_async_remote_copy(
            src_ref=src.at[part(i)],
            dst_ref=dst.at[way, part(i)],
            send_sem=send.at[way, i],
            recv_sem=recv.at[way, i],
            device_id=ahead if way == 0 else behind,
            device_id_type=MESH,
        )

    def push_p(way, i):
        return push(send_p.at[way], recv_p, p_send, p_recv, way, i)

    def push_g(way, i):
        return push(gc, recv_g, g_send, g_recv, way, i)

    def forward(i):
        load_act(i).wait()

        def norm(j, _):
            at = pl.ds(pl.multiple_of(i * CHUNK + j * SUB, SUB), SUB)
            v = act[at].astype(F32)
            r = lax.rsqrt(jnp.mean(v * v, axis=-1, keepdims=True) + EPS)
            u = v * r * gain_in[...]
            _, t = tanh_part(u)
            hid[at] = (0.5 * u * (1.0 + t)).astype(BF16)
            return 0

        lax.fori_loop(0, CHUNK // SUB, norm, 0)

    def products(i):
        send_p[0, part(i)] = nn_dot(hid[part(i)], tap[0]).astype(BF16)
        push_p(0, i).start()
        send_p[1, part(i)] = nn_dot(hid[part(i)], tap[2]).astype(BF16)
        push_p(1, i).start()

    loads[1].wait()
    forward(0)
    loads[2].wait()
    loads[3].wait()
    pl.semaphore_wait(barrier, n_place - 1 + n1 - 1)
    products(0)

    def first(i, _):
        forward(i)
        products(i)
        return 0

    lax.fori_loop(1, n, first, 0)

    for k in (0, 4, 5, 6, 7):
        loads[k].wait()
    acc_in[...] = jnp.zeros_like(acc_in)
    acc_mid[...] = jnp.zeros_like(acc_mid)

    def inner(i, _):
        cen[part(i)] = nn_dot(hid[part(i)], tap[1])
        gmid[part(i)] = nt_dot(ct[part(i)], point[...])
        return 0

    lax.fori_loop(0, n, inner, 0)

    bounds = []
    for k in range(lengths.shape[1]):
        bounds.append(lengths[0, k] + (bounds[-1] if bounds else 0))

    def owner(pos):
        return sum((pos >= b).astype(jnp.int32) for b in bounds)

    def valid(start, size):
        pos = seq * rows + start + lax.broadcasted_iota(jnp.int32, (size, 1), 0)
        own = owner(pos)
        before = jnp.where((pos >= reach) & (owner(pos - reach) == own), 1.0, 0.0)
        after = jnp.where((pos < total - reach) & (owner(pos + reach) == own), 1.0, 0.0)
        return before.astype(F32), after.astype(F32)

    def fold(x):
        return x[:8] + x[8:]

    def middle(i, _):
        push_p(0, i).wait_recv()
        push_p(1, i).wait_recv()

        def step(j, _):
            start = pl.multiple_of(i * CHUNK + j * SUB, SUB)
            at = pl.ds(start, SUB)
            before, after = valid(start, SUB)
            v = cen[at] + before * recv_p[0, at].astype(F32) + after * recv_p[1, at].astype(F32)
            r = lax.rsqrt(jnp.mean(v * v, axis=-1, keepdims=True) + EPS)
            nv = v * r
            u = nv * gain_mid[...]
            u2, t = tanh_part(u)
            mid[at] = (0.5 * u * (1.0 + t)).astype(BF16)
            du = gmid[at] * slope(u, u2, t)
            dun = du * nv
            acc_mid[...] += fold(dun)
            s = jnp.mean(dun * gain_mid[...], axis=-1, keepdims=True)
            gc[at] = (r * (du * gain_mid[...] - nv * s)).astype(BF16)
            return 0

        lax.fori_loop(0, CHUNK // SUB, step, 0)
        push_g(0, i).start()
        push_g(1, i).start()
        out[part(i)] = (
            act[part(i)].astype(F32) + nn_dot(mid[part(i)], point[...])
        ).astype(BF16)
        pltpu.make_async_copy(out.at[part(i)], out_hbm.at[0, part(i)], out_sem.at[i]).start()
        gh[part(i)] = nt_dot(gc[part(i)], tap[1])
        return 0

    lax.fori_loop(0, n, middle, 0)

    def backward(i, _):
        push_g(0, i).wait_recv()
        push_g(1, i).wait_recv()
        before, after = valid(pl.multiple_of(i * CHUNK, CHUNK), CHUNK)
        gb = (recv_g[0, part(i)].astype(F32) * before).astype(BF16)
        ga = (recv_g[1, part(i)].astype(F32) * after).astype(BF16)
        gh[part(i)] += nt_dot(gb, tap[2]) + nt_dot(ga, tap[0])

        def step(j, _):
            start = pl.multiple_of(i * CHUNK + j * SUB, SUB)
            at = pl.ds(start, SUB)
            v = act[at].astype(F32)
            r = lax.rsqrt(jnp.mean(v * v, axis=-1, keepdims=True) + EPS)
            nv = v * r
            u = nv * gain_in[...]
            u2, t = tanh_part(u)
            du = gh[at] * slope(u, u2, t)
            dun = du * nv
            acc_in[...] += fold(dun)
            s = jnp.mean(dun * gain_in[...], axis=-1, keepdims=True)
            dv = r * (du * gain_in[...] - nv * s)
            ing[at] = (ct[at].astype(F32) + dv).astype(BF16)
            return 0

        lax.fori_loop(0, CHUNK // SUB, step, 0)
        pltpu.make_async_copy(ing.at[part(i)], ing_hbm.at[0, part(i)], ing_sem.at[i]).start()
        return 0

    lax.fori_loop(0, n, backward, 0)

    def exchange(slots, me, peer, count, send, recv):
        def copy(k):
            j, device = peer(k)
            return pltpu.make_async_remote_copy(
                src_ref=slots.at[me],
                dst_ref=slots.at[me],
                send_sem=send.at[j],
                recv_sem=recv.at[me],
                device_id=device,
                device_id_type=MESH,
            )

        def arrival(k):
            j, device = peer(k)
            return pltpu.make_async_remote_copy(
                src_ref=slots.at[j],
                dst_ref=slots.at[j],
                send_sem=send.at[j],
                recv_sem=recv.at[j],
                device_id=device,
                device_id_type=MESH,
            )

        for k in range(1, count):
            copy(k).start()
        for k in range(1, count):
            arrival(k).wait_recv()
        summed = slots[0]
        for k in range(1, count):
            summed = summed + slots[k]
        return summed, copy

    slots1[me1, :, :c] = jnp.sum(acc_in[...], axis=0, keepdims=True)
    slots1[me1, :, c:] = jnp.sum(acc_mid[...], axis=0, keepdims=True)
    summed, copy1 = exchange(slots1, me1, peer1, n1, r1_send, r1_recv)
    slots2[place] = summed
    summed, copy2 = exchange(slots2, place, peer2, n_place, r2_send, r2_recv)
    summed = summed * (1.0 / math.sqrt(n_batch * total))
    gsum_in[...] = summed[:, :c]
    gsum_mid[...] = summed[:, c:]

    for k in range(1, n1):
        copy1(k).wait_send()
    for k in range(1, n_place):
        copy2(k).wait_send()
    for i in range(n):
        for way in range(2):
            push_p(way, i).wait_send()
            push_g(way, i).wait_send()
        pltpu.make_async_copy(out.at[part(i)], out_hbm.at[0, part(i)], out_sem.at[i]).wait()
        pltpu.make_async_copy(ing.at[part(i)], ing_hbm.at[0, part(i)], ing_sem.at[i]).wait()


def body(
    n_seq, n_batch,
    activations, cotangent, contig_lengths, gain_input, tap_weights, gain_middle, point_weights,
):
    _, rows, c = activations.shape
    f = tap_weights.shape[2]
    n = rows // CHUNK
    n1 = CORES * n_batch
    n2 = n_seq // CORES
    vmem = pltpu.VMEM
    dma = pltpu.SemaphoreType.DMA
    anywhere = pl.BlockSpec(memory_space=pl.ANY)
    whole = pl.BlockSpec(memory_space=vmem)
    result = pl.pallas_call(
        functools.partial(kernel, n_seq, n_batch),
        name="block",
        out_shape=[
            jax.ShapeDtypeStruct((1, rows, c), BF16),
            jax.ShapeDtypeStruct((1, rows, c), BF16),
            jax.ShapeDtypeStruct((1, c), F32),
            jax.ShapeDtypeStruct((1, f), F32),
        ],
        in_specs=[anywhere] * 7,
        out_specs=[anywhere, anywhere, whole, whole],
        scratch_shapes=[
            pltpu.SMEM(contig_lengths.shape, jnp.int32),
            vmem((rows, c), BF16),
            vmem((rows, c), BF16),
            vmem((1, c), F32),
            vmem((3, c, f), BF16),
            vmem((1, f), F32),
            vmem((f, c), BF16),
            vmem((rows, c), BF16),
            vmem((2, rows, f), BF16),
            vmem((2, rows, f), BF16),
            vmem((rows, f), F32),
            vmem((rows, f), F32),
            vmem((rows, f), BF16),
            vmem((2, rows, f), BF16),
            vmem((rows, f), BF16),
            vmem((rows, c), F32),
            vmem((rows, c), BF16),
            vmem((rows, c), BF16),
            vmem((8, c), F32),
            vmem((8, f), F32),
            vmem((n1, 1, c + f), F32),
            vmem((n2, 1, c + f), F32),
            dma((8,)),
            dma((n,)),
            dma((n,)),
            dma((n,)),
            dma((2, n)),
            dma((2, n)),
            dma((2, n)),
            dma((2, n)),
            dma((n1,)),
            dma((n1,)),
            dma((n2,)),
            dma((n2,)),
        ],
        compiler_params=pltpu.CompilerParams(
            collective_id=0, has_side_effects=True, vmem_limit_bytes=48 * 2**20
        ),
        cost_estimate=pl.CostEstimate(
            flops=16 * rows * c * f, bytes_accessed=16 * 2**20, transcendentals=3 * rows * c
        ),
    )(
        contig_lengths,
        activations,
        cotangent,
        gain_input.reshape(1, c),
        tap_weights,
        gain_middle.reshape(1, f),
        point_weights,
    )
    out, ing, gsum_in, gsum_mid = result
    return out, ing, gsum_in.reshape(c), gsum_mid.reshape(f)


def solution(mesh):
    placed = (
        P("batch", "seq", None),
        P("batch", "seq", None),
        P("batch", None),
        P(),
        P(),
        P(),
        P(),
    )
    return jax.shard_map(
        functools.partial(body, mesh.shape["seq"], mesh.shape["batch"]),
        mesh=mesh,
        in_specs=placed,
        out_specs=(P("batch", "seq", None), P("batch", "seq", None), P(), P()),
        check_vma=False,
    )
```

time: 263 us -> 106 us (0.40)
  waiting for transfers between devices: 130 us -> 0 us
  Pallas kernels: 0 us -> 98.2 us
  blocking collectives: 78.7 us -> 0 us
  matrix products: 26.1 us -> 0 us
  starting transfers between devices: 15.2 us -> 0 us
  other arithmetic: 11.9 us -> 1.22 us
  local copies, waits for them, and re-layouts: 0.24 us -> 5.74 us
    ppermute x4 -> x0, waiting for transfers between devices: 130 us -> none  [shifted(): return lax.ppermute(x, axis, pairs)]
    pallas_call x0 -> x1, Pallas kernels: none -> 98.2 us  [body(): pl.pallas_call(functools.partial(kernel, n_seq, n_batch), name='block', o...]
    psum x1 -> x0, blocking collectives: 78.7 us -> none  [body(): summed = lax.psum((input_terms, middle_terms), ('seq', 'batch'))]
    dot_general x8 -> x0, matrix products: 26.1 us -> none  [the longest x1 6.11 us: body(): jnp.dot(grad_combined, tap_center.T, preferred_element_type=jnp.float32)]
    ppermute x4 -> x0, starting transfers between devices: 15.2 us -> none  [shifted(): return lax.ppermute(x, axis, pairs)]
    broadcast_in_dim x1 -> x0, other arithmetic: 4.9 us -> none  [body(): grad_output[None]]
    unnamed x18 -> x6, local copies, waits for them, and re-layouts: 0.24 us -> 4.35 us
    convert_element_type x3 -> x0, other arithmetic: 3.58 us -> none  [the longest x1 3.21 us: body(): hidden = normed.astype(jnp.bfloat16)]
  transfers between devices with their start and end apart: 4 -> 0, of which waited for: 4 -> 0; matrix products, arithmetic and copies ran while one was open for 4% -> 0% of each run, Pallas kernels for 0% -> 0%
where the time goes in v1:
time: 106 us
  Pallas kernels  98.2 us (93%)
  local copies, waits for them, and re-layouts  5.74 us (5%)
  other arithmetic  1.22 us (1%)
    pallas_call x1, Pallas kernels, body(): pl.pallas_call(functools.partial(kernel, n_seq, n_batch), name='block', o...  98.2 us
    unnamed x6, local copies, waits for them, and re-layouts  4.35 us

profile of v1, /device:TPU:1, one launch (start us, length us, event | category | flops | bytes accessed | tf_op | source)
XLA Modules:
  0.0 105.8 jit_solution(6838176285017078006)
XLA Ops:
  0.6 0.7 reshape.20.gain_in_hbm
  1.3 0.7 reshape.21.gain_mid_hbm
  2.0 0.0 copy-start
  2.0 1.4 %copy-done = bf16[1,512,1536]{2,1,0:T(8,128)(2,1)S(1)} copy-done((bf16[1,512,1536]{2,1,0:T(8,128)(2,1)S(1)}, bf16[1,512,1536]{2,1,0:T(8,128)(2,1)}, u32[]{:S(2)}) %copy-start) | copy-done | bytes 1572888
  3.4 0.0 copy-start.1
  3.4 0.7 copy-done.1
  4.1 98.2 %block.1 = (bf16[1,512,1536]{2,1,0:T(8,128)(2,1)S(1)}, bf16[1,512,1536]{2,1,0:T(8,128)(2,1)S(1)}, f32[1,1536]{1,0:T(1,128)S(1)}, f32[1,768]{1,0:T(1,128)S(1)}) custom-call(s32[1,4]{1,0:T(1,128)S(1)} %copy-done.1, bf16[1,512,1536]{2,1,0:T(8,128)(2,1)S(1)} %copy-done, bf16[1,512,1536]{2,1,0:T(8,128)(2,1)} %ct_hbm.1, f32[1,1536]{1,0:T(1,128)S(1)} %reshape.20.gain_in_hbm, ...), custom_call_target="tpu_custom_call" | custom-call | flops 9663676416 | bytes 16777216 | tf_op jit(solution)/shard_map/block/pallas_call | solution.py:312
  102.3 0.6 reduce
  102.9 0.6 reduce.1
  103.5 1.1 %copy.13 = bf16[1,512,1536]{2,1,0:T(8,128)(2,1)} copy(bf16[1,512,1536]{2,1,0:T(8,128)(2,1)S(1)} %get-tuple-element.16) | data formatting | bytes 3145728
  104.7 1.1 %copy.14 = bf16[1,512,1536]{2,1,0:T(8,128)(2,1)} copy(bf16[1,512,1536]{2,1,0:T(8,128)(2,1)S(1)} %get-tuple-element.17) | data formatting | bytes 3145728
Async XLA Ops:
  2.0 1.4 %copy-start = (bf16[1,512,1536]{2,1,0:T(8,128)(2,1)S(1)}, bf16[1,512,1536]{2,1,0:T(8,128)(2,1)}, u32[]{:S(2)}) copy-start(bf16[1,512,1536]{2,1,0:T(8,128)(2,1)} %act_hbm.1) | copy-start | bytes 4718596
  3.4 0.7 copy-start.1

commit v2 on v0

v2 whole, which is shorter than its diff:
```python
import functools
import math

import jax
import jax.numpy as jnp
from jax import lax
from jax.experimental import pallas as pl
from jax.experimental.pallas import tpu as pltpu
from jax.sharding import PartitionSpec as P

SPAN = 2
CORES = 2
EPS = 1e-06
ROOT = math.sqrt(2.0 / math.pi)
CUBIC = 0.044715
SUB = 16
TILE = 256
GROUPS = ((0, 64, 1), (64, 64, 1), (128, 128, 2), (384, 64, 2))
RAW = 16
LANES = 128
MESH = pl.DeviceIdType.MESH
F32 = jnp.float32
BF16 = jnp.bfloat16
EXTENT = {"core": 2, "x": 4, "y": 4, "z": 8}
STAGES = (("core",), ("x", "y"), ("z",))
STAGE_SIZES = tuple(math.prod(EXTENT[a] for a in axes) for axes in STAGES)


def tanh_part(u):
    u2 = u * u
    return u2, jnp.tanh(ROOT * u * (1.0 + CUBIC * u2))


def slope(u, u2, t):
    return 0.5 * (1.0 + t) + 0.5 * u * (1.0 - t * t) * (ROOT * (1.0 + 3.0 * CUBIC * u2))


def nt_dot(a, b):
    return lax.dot_general(a, b, (((1,), (1,)), ((), ())), preferred_element_type=F32)


def nn_dot(a, b):
    return jnp.dot(a, b, preferred_element_type=F32)


def fold(x):
    return x[:8] + x[8:]


def kernel(
    n_seq, n_batch, n_contig,
    small, act_hbm, ct_hbm, tap_hbm, point_hbm,
    out_hbm, ing_hbm, gsum_in, gsum_mid,
    act, ct, tap, point, before, after,
    hid, raw, raw_hid, send_p, recv_p, cen, gmid, gc, recv_g, mid, gh, slp, inv, out, ing,
    gain_in_b, gain_mid_b, acc_in, acc_mid, packed, slots0, slots1, slots2,
    in_sem, act_sem, out_sem, ing_sem, raw_send, raw_recv,
    p_send, p_recv, g_send, g_recv,
    send0, send1, send2, got0, got1, got2,
):
    slots, ex_send, ex_got = (slots0, slots1, slots2), (send0, send1, send2), (got0, got1, got2)
    rows, c = act.shape
    f = mid.shape[1]
    reach = SPAN * rows
    total = rows * n_seq
    seq = lax.axis_index("seq")
    batch = lax.axis_index("batch")
    half_z = EXTENT["z"] // 2
    here = {
        "core": lax.rem(seq, CORES),
        "x": seq // (CORES * half_z),
        "y": lax.rem(batch, EXTENT["y"]),
        "z": lax.rem(seq // CORES, half_z) * 2 + batch // EXTENT["y"],
    }

    def device(at):
        return {
            "seq": (at["x"] * half_z + at["z"] // 2) * CORES + at["core"],
            "batch": lax.rem(at["z"], 2) * EXTENT["y"] + at["y"],
        }

    def group(axes):
        size = math.prod(EXTENT[a] for a in axes)
        me = 0
        for a in axes:
            me = me * EXTENT[a] + here[a]

        def peer(k):
            j = lax.rem(me + k, size)
            at, left = dict(here), j
            for a in reversed(axes):
                at[a] = lax.rem(left, EXTENT[a])
                left = left // EXTENT[a]
            return j, device(at)

        return size, me, peer

    ahead = {"seq": lax.rem(seq + SPAN, n_seq), "batch": batch}
    behind = {"seq": lax.rem(seq + n_seq - SPAN, n_seq), "batch": batch}
    stages = [group(axes) for axes in STAGES]

    def span(base, size, i):
        return pl.ds(pl.multiple_of(base + i * size, size), size)

    def load_act(k, at):
        return pltpu.make_async_copy(act_hbm.at[0, at], act.at[at], act_sem.at[k])

    load_tap = [pltpu.make_async_copy(tap_hbm.at[k], tap.at[k], in_sem.at[k]) for k in range(3)]
    load_point = pltpu.make_async_copy(point_hbm, point, in_sem.at[3])
    load_ct = pltpu.make_async_copy(ct_hbm.at[0], ct, in_sem.at[4])
    lead = GROUPS[0][1]
    load_first = load_act(0, pl.ds(0, lead))
    load_rest = load_act(1, pl.ds(lead, rows - lead))
    load_first.start()
    load_tap[0].start()
    load_tap[2].start()

    barrier = pltpu.get_barrier_semaphore()
    greeted = [ahead, behind]
    for size, _, peer in stages:
        greeted += [peer(k)[1] for k in range(1, size)]
    for d in greeted:
        pl.semaphore_signal(barrier, inc=1, device_id=d, device_id_type=MESH)

    def push(src, dst, send, recv, way, k, at):
        return pltpu.make_async_remote_copy(
            src_ref=src.at[at],
            dst_ref=dst.at[way, at],
            send_sem=send.at[way, k],
            recv_sem=recv.at[way, k],
            device_id=behind if way else ahead,
            device_id_type=MESH,
        )

    def push_p(way, k, at):
        return push(send_p.at[way], recv_p, p_send, p_recv, way, k, at)

    def push_g(way, k, at):
        return push(gc, recv_g, g_send, g_recv, way, k, at)

    def each_chunk(fn, groups=GROUPS, first=0):
        for base, size, count in groups:

            def one(i, _, base=base, size=size, first=first):
                fn(first + i, pl.multiple_of(base + i * size, size), size)
                return 0

            if count == 1:
                fn(first, base, size)
            else:
                lax.fori_loop(0, count, one, 0)
            first += count

    def each_sub(start, size, fn, unroll=2):
        def one(j, _):
            fn(pl.ds(pl.multiple_of(start + j * SUB, SUB), SUB), start + j * SUB)
            return 0

        lax.fori_loop(0, size // SUB, one, 0, unroll=unroll)

    def norm(at, _):
        v = act[at].astype(F32)
        r = lax.rsqrt(jnp.mean(v * v, axis=-1, keepdims=True) + EPS)
        u = v * r * gain_in_b[...]
        _, t = tanh_part(u)
        inv[at] = r
        hid[at] = (0.5 * u * (1.0 + t)).astype(BF16)

    def product(way, k, at):
        send_p[way, at] = nn_dot(hid[at], tap[2 * way]).astype(BF16)
        push_p(way, k, at).start()

    def push_raw(way):
        return pltpu.make_async_remote_copy(
            src_ref=act_hbm.at[0, pl.ds(0, RAW)],
            dst_ref=raw.at[way],
            send_sem=raw_send.at[way],
            recv_sem=raw_recv.at[way],
            device_id=behind if way else ahead,
            device_id_type=MESH,
        )

    def product_rows(k, start, size):
        return pl.ds(RAW, size - RAW) if isinstance(k, int) and k == 0 else pl.ds(start, size)

    gain_in_b[...] = jnp.broadcast_to(small[pl.ds(0, c)].reshape(1, c), (SUB, c))
    load_first.wait()
    each_sub(0, lead, norm)
    pl.semaphore_wait(barrier, len(greeted))
    push_raw(0).start()
    push_raw(1).start()
    load_tap[0].wait()
    product(0, 0, product_rows(0, 0, lead))
    load_tap[2].wait()
    product(1, 0, product_rows(0, 0, lead))
    load_rest.start()
    load_tap[1].start()
    load_point.start()
    load_ct.start()
    load_rest.wait()

    def forward(k, start, size):
        each_sub(start, size, norm)
        product(0, k, pl.ds(start, size))
        product(1, k, pl.ds(start, size))

    each_chunk(forward, GROUPS[1:], 1)

    load_tap[1].wait()
    load_point.wait()
    load_ct.wait()
    gain_mid_b[...] = jnp.broadcast_to(small[pl.ds(c, f)].reshape(1, f), (SUB, f))
    acc_in[...] = jnp.zeros_like(acc_in)
    acc_mid[...] = jnp.zeros_like(acc_mid)

    def tiles(width, fn):
        def one(i, _):
            fn(pl.ds(pl.multiple_of(i * TILE, TILE), TILE))
            return 0

        lax.fori_loop(0, width // TILE, one, 0)

    def inner(at):
        cen[:, at] = nn_dot(hid[...], tap[1, :, at])
        gmid[:, at] = nt_dot(ct[...], point[at])

    tiles(f, inner)

    lengths = small[pl.ds(c + f, LANES)].reshape(1, LANES)
    bounds = []
    for k in range(n_contig):
        bounds.append(lengths[:, k : k + 1] + (bounds[-1] if bounds else 0.0))

    def owner(pos):
        return sum((pos >= b).astype(F32) for b in bounds)

    def valid(at, row):
        pos = (seq * rows + row + lax.broadcasted_iota(jnp.int32, (SUB, 1), 0)).astype(F32)
        own = owner(pos)
        before[at] = jnp.where((pos >= reach) & (owner(pos - reach) == own), 1.0, 0.0)
        after[at] = jnp.where((pos < total - reach) & (owner(pos + reach) == own), 1.0, 0.0)

    each_sub(0, rows, valid)

    for way in range(2):
        push_raw(way).wait_recv()
        v = raw[way].astype(F32)
        u = v * lax.rsqrt(jnp.mean(v * v, axis=-1, keepdims=True) + EPS) * gain_in_b[...]
        raw_hid[...] = (0.5 * u * (1.0 + tanh_part(u)[1])).astype(BF16)
        recv_p[way, pl.ds(0, RAW)] = nn_dot(raw_hid[...], tap[2 * way]).astype(BF16)

    def exchange(slots, send, got, stage):
        count, me, peer = stage
        order = sorted(range(1, count), key=lambda k: -min(k, count - k))

        def copy(k, j, device_id):
            return pltpu.make_async_remote_copy(
                src_ref=slots.at[j],
                dst_ref=slots.at[j],
                send_sem=send.at[k],
                recv_sem=got.at[j],
                device_id=device_id,
                device_id_type=MESH,
            )

        def begin(value):
            slots[me] = value
            for k in order:
                copy(k, me, peer(k)[1]).start()

        def finish():
            for k in order:
                copy(k, *peer(k)).wait_recv()
            summed = slots[0]
            for k in range(1, count):
                summed = summed + slots[k]
            return summed

        def settle():
            for k in order:
                copy(k, me, peer(k)[1]).wait_send()

        return begin, finish, settle

    gain_stages = [exchange(*part) for part in zip(slots, ex_send, ex_got, stages)]
    scale = 1.0 / math.sqrt(n_batch * total)

    def middle(k, start, size):
        chunk = pl.ds(start, size)
        for way in range(2):
            push_p(way, k, product_rows(k, start, size)).wait_recv()

        def step(at, _):
            v = (
                cen[at]
                + before[at] * recv_p[0, at].astype(F32)
                + after[at] * recv_p[1, at].astype(F32)
            )
            r = lax.rsqrt(jnp.mean(v * v, axis=-1, keepdims=True) + EPS)
            nv = v * r
            u = nv * gain_mid_b[...]
            u2, t = tanh_part(u)
            mid[at] = (0.5 * u * (1.0 + t)).astype(BF16)
            du = gmid[at] * slope(u, u2, t)
            dun = du * nv
            acc_mid[...] += fold(dun)
            s = jnp.mean(dun * gain_mid_b[...], axis=-1, keepdims=True)
            gc[at] = (r * (du * gain_mid_b[...] - nv * s)).astype(BF16)

        each_sub(start, size, step)
        push_g(0, k, chunk).start()
        push_g(1, k, chunk).start()

    each_chunk(middle)

    def block(at):
        out[:, at] = (act[:, at].astype(F32) + nn_dot(mid[...], point[:, at])).astype(BF16)
        gh[:, at] = nt_dot(gc[...], tap[1, at])

    tiles(c, block)
    write_out = pltpu.make_async_copy(out, out_hbm.at[0], out_sem.at[0])
    write_out.start()

    def slopes(at, _):
        u = act[at].astype(F32) * inv[at] * gain_in_b[...]
        u2, t = tanh_part(u)
        slp[at] = slope(u, u2, t)

    each_sub(0, rows, slopes)

    def arrive(k, start, size):
        at = pl.ds(start, size)
        push_g(0, k, at).wait_recv()
        gb = (recv_g[0, at].astype(F32) * before[at]).astype(BF16)
        gh[at] += nt_dot(gb, tap[2])
        push_g(1, k, at).wait_recv()
        ga = (recv_g[1, at].astype(F32) * after[at]).astype(BF16)
        gh[at] += nt_dot(ga, tap[0])

    def terms(at, _):
        acc_in[...] += fold(gh[at] * slp[at] * (act[at].astype(F32) * inv[at]))

    def input_grad(at, _):
        r = inv[at]
        nv = act[at].astype(F32) * r
        dug = gh[at] * slp[at] * gain_in_b[...]
        s = jnp.mean(dug * nv, axis=-1, keepdims=True)
        ing[at] = (ct[at].astype(F32) + r * (dug - nv * s)).astype(BF16)

    def backward(k, start, size):
        arrive(k, start, size)
        each_sub(start, size, terms)
        each_sub(start, size, input_grad)

    base, size, count = GROUPS[-1]
    chunks = sum(g[2] for g in GROUPS)
    each_chunk(backward, GROUPS[:-1] + ((base, size, count - 1),))
    early = pl.ds(0, rows - size)
    late = pl.ds(rows - size, size)
    write_early = pltpu.make_async_copy(ing.at[early], ing_hbm.at[0, early], ing_sem.at[0])
    write_late = pltpu.make_async_copy(ing.at[late], ing_hbm.at[0, late], ing_sem.at[1])
    write_early.start()
    arrive(chunks - 1, rows - size, size)
    each_sub(rows - size, size, terms)

    lines = (c + f) // LANES
    for acc, base in ((acc_in, 0), (acc_mid, c // LANES)):
        line = jnp.sum(acc[...], axis=0, keepdims=True)
        for i in range(acc.shape[1] // LANES):
            packed[pl.ds(base + i, 1)] = line[:, i * LANES : (i + 1) * LANES]
    gain_stages[0][0](packed[...])
    gain_stages[1][0](gain_stages[0][1]())
    gain_stages[2][0](gain_stages[1][1]())
    each_sub(rows - size, size, input_grad)
    write_late.start()
    for stage in gain_stages[:2]:
        stage[2]()

    def sent(k, start, size):
        at = pl.ds(start, size)
        for way in range(2):
            push_p(way, k, product_rows(k, start, size)).wait_send()
            push_g(way, k, at).wait_send()

    each_chunk(sent)
    push_raw(0).wait_send()
    push_raw(1).wait_send()
    write_out.wait()
    write_early.wait()
    summed = gain_stages[2][1]() * scale
    for i in range(lines):
        to, j = (gsum_in, i) if i < c // LANES else (gsum_mid, i - c // LANES)
        to[pl.ds(j * LANES, LANES)] = summed[i]
    gain_stages[2][2]()
    write_late.wait()


def finish_kernel(out, ing, gsum_in, gsum_mid, out_to, ing_to, gsum_in_to, gsum_mid_to, sems):
    copies = [
        pltpu.make_async_copy(out, out_to, sems.at[0]),
        pltpu.make_async_copy(ing, ing_to, sems.at[1]),
    ]
    for copy in copies:
        copy.start()
    gsum_in_to[...] = gsum_in[...]
    gsum_mid_to[...] = gsum_mid[...]
    for copy in copies:
        copy.wait()


def body(
    n_seq, n_batch,
    activations, cotangent, contig_lengths, gain_input, tap_weights, gain_middle, point_weights,
):
    _, rows, c = activations.shape
    f = tap_weights.shape[2]
    n = sum(g[2] for g in GROUPS)
    vmem = pltpu.VMEM
    dma = pltpu.SemaphoreType.DMA
    anywhere = pl.BlockSpec(memory_space=pl.ANY)
    hbm = pl.BlockSpec(memory_space=pltpu.HBM)
    whole = pl.BlockSpec(memory_space=vmem)
    shapes = [
        jax.ShapeDtypeStruct((1, rows, c), BF16),
        jax.ShapeDtypeStruct((1, rows, c), BF16),
        jax.ShapeDtypeStruct((c,), F32),
        jax.ShapeDtypeStruct((f,), F32),
    ]
    lengths = jnp.pad(contig_lengths[0].astype(F32), (0, LANES - contig_lengths.shape[1]))
    small = jnp.concatenate([gain_input, gain_middle, lengths])
    result = pl.pallas_call(
        functools.partial(kernel, n_seq, n_batch, contig_lengths.shape[1]),
        name="block",
        out_shape=shapes,
        in_specs=[whole] + [hbm] * 4,
        out_specs=[anywhere, anywhere, whole, whole],
        scratch_shapes=[
            vmem((rows, c), BF16),
            vmem((rows, c), BF16),
            vmem((3, c, f), BF16),
            vmem((f, c), BF16),
            vmem((rows, 1), F32),
            vmem((rows, 1), F32),
            vmem((rows, c), BF16),
            vmem((2, RAW, c), BF16),
            vmem((RAW, c), BF16),
            vmem((2, rows, f), BF16),
            vmem((2, rows, f), BF16),
            vmem((rows, f), F32),
            vmem((rows, f), F32),
            vmem((rows, f), BF16),
            vmem((2, rows, f), BF16),
            vmem((rows, f), BF16),
            vmem((rows, c), F32),
            vmem((rows, c), F32),
            vmem((rows, 1), F32),
            vmem((rows, c), BF16),
            vmem((rows, c), BF16),
            vmem((SUB, c), F32),
            vmem((SUB, f), F32),
            vmem((8, c), F32),
            vmem((8, f), F32),
        ]
        + [vmem(((c + f) // LANES, LANES), F32)]
        + [vmem((size, (c + f) // LANES, LANES), F32) for size in STAGE_SIZES]
        + [dma((5,)), dma((2,)), dma((1,)), dma((2,)), dma((2,)), dma((2,))]
        + [dma((2, n))] * 4
        + [dma((size,)) for size in STAGE_SIZES] * 2,
        compiler_params=pltpu.CompilerParams(
            collective_id=0, has_side_effects=True, vmem_limit_bytes=50 * 2**20
        ),
        cost_estimate=pl.CostEstimate(
            flops=16 * rows * c * f, bytes_accessed=16 * 2**20, transcendentals=3 * rows * c
        ),
    )(
        small, activations, cotangent, tap_weights, point_weights
    )
    out, ing, gsum_in, gsum_mid = pl.pallas_call(
        finish_kernel,
        name="tail",
        out_shape=shapes,
        in_specs=[anywhere, anywhere, whole, whole],
        out_specs=[hbm, hbm, whole, whole],
        scratch_shapes=[dma((2,))],
        compiler_params=pltpu.CompilerParams(vmem_limit_bytes=8 * 2**20),
    )(*result)
    return out, ing, gsum_in, gsum_mid


def solution(mesh):
    placed = (
        P("batch", "seq", None),
        P("batch", "seq", None),
        P("batch", None),
        P(),
        P(),
        P(),
        P(),
    )
    return jax.shard_map(
        functools.partial(body, mesh.shape["seq"], mesh.shape["batch"]),
        mesh=mesh,
        in_specs=placed,
        out_specs=(P("batch", "seq", None), P("batch", "seq", None), P(), P()),
        check_vma=False,
    )
```

time: 263 us -> 100 us (0.38)
  waiting for transfers between devices: 130 us -> 0 us
  Pallas kernels: 0 us -> 98.2 us
  blocking collectives: 78.7 us -> 0 us
  matrix products: 26.1 us -> 0 us
  starting transfers between devices: 15.2 us -> 0 us
  other arithmetic: 11.9 us -> 1.38 us
    ppermute x4 -> x0, waiting for transfers between devices: 130 us -> none  [shifted(): return lax.ppermute(x, axis, pairs)]
    pallas_call x0 -> x2, Pallas kernels: none -> 98.2 us  [the longest x1 95.9 us: body(): pl.pallas_call(functools.partial(kernel, n_seq, n_batch, contig_lengths.s...]
    psum x1 -> x0, blocking collectives: 78.7 us -> none  [body(): summed = lax.psum((input_terms, middle_terms), ('seq', 'batch'))]
    dot_general x8 -> x0, matrix products: 26.1 us -> none  [the longest x1 6.11 us: body(): jnp.dot(grad_combined, tap_center.T, preferred_element_type=jnp.float32)]
    ppermute x4 -> x0, starting transfers between devices: 15.2 us -> none  [shifted(): return lax.ppermute(x, axis, pairs)]
    broadcast_in_dim x1 -> x0, other arithmetic: 4.9 us -> none  [body(): grad_output[None]]
    convert_element_type x3 -> x1, other arithmetic: 3.58 us -> 0.66 us  [body(): contig_lengths[0].astype(F32)]
  transfers between devices with their start and end apart: 4 -> 0, of which waited for: 4 -> 0; matrix products, arithmetic and copies ran while one was open for 4% -> 0% of each run, Pallas kernels for 0% -> 0%
where the time goes in v2:
time: 100 us
  Pallas kernels  98.2 us (98%)
  other arithmetic  1.38 us (1%)
    pallas_call x1, Pallas kernels, body(): pl.pallas_call(functools.partial(kernel, n_seq, n_batch, contig_lengths.s...  95.9 us
    pallas_call x1, Pallas kernels, body(): pl.pallas_call(finish_kernel, name='tail', out_shape=shapes, in_specs=[an...  2.27 us

profile of v2, /device:TPU:1, one launch (start us, length us, event | category | flops | bytes accessed | tf_op | source)
XLA Modules:
  0.0 100.2 jit_solution(3714850351058292765)
XLA Ops:
  0.6 0.7 convert_bitcast_fusion
  1.3 0.7 select_maximum_fusion.small
  2.0 95.9 %block.1 = (bf16[1,512,1536]{2,1,0:T(8,128)(2,1)S(1)}, bf16[1,512,1536]{2,1,0:T(8,128)(2,1)S(1)}, f32[1536]{0:T(1024)S(1)}, f32[768]{0:T(1024)S(1)}) custom-call(f32[2432]{0:T(1024)S(1)} %select_maximum_fusion.small, bf16[1,512,1536]{2,1,0:T(8,128)(2,1)} %act_hbm.1, bf16[1,512,1536]{2,1,0:T(8,128)(2,1)} %ct_hbm.1, bf16[3,1536,768]{2,1,0:T(8,128)(2,1)} %tap_hbm.1, ...), custom_call_target="tpu_custom_call" | custom-call | flops 9663676416 | bytes 16777216 | tf_op jit(solution)/shard_map/block/pallas_call | solution.py:431
  97.9 2.3 %tail.1 = (bf16[1,512,1536]{2,1,0:T(8,128)(2,1)}, bf16[1,512,1536]{2,1,0:T(8,128)(2,1)}, f32[1536]{0:T(1024)}, f32[768]{0:T(1024)}) custom-call(bf16[1,512,1536]{2,1,0:T(8,128)(2,1)S(1)} %get-tuple-element.8.out, bf16[1,512,1536]{2,1,0:T(8,128)(2,1)S(1)} %get-tuple-element.9.ing, f32[1536]{0:T(1024)S(1)} %get-tuple-element.10.gsum_in, ...), custom_call_target="tpu_custom_call" | custom-call | tf_op jit(solution)/shard_map/tail/pallas_call | solution.py:478

commit v3 on v2

--- a/solution.py
+++ b/solution.py
@@ -15,7 +15,7 @@
 CUBIC = 0.044715
 SUB = 16
 TILE = 256
-GROUPS = ((0, 64, 1), (64, 64, 1), (128, 128, 2), (384, 64, 2))
+GROUPS = ((0, 64, 1), (64, 64, 1), (128, 128, 3))
 RAW = 16
 LANES = 128
 MESH = pl.DeviceIdType.MESH
@@ -51,7 +51,7 @@
     n_seq, n_batch, n_contig,
     small, act_hbm, ct_hbm, tap_hbm, point_hbm,
     out_hbm, ing_hbm, gsum_in, gsum_mid,
-    act, ct, tap, point, before, after,
+    act, ct, tap, tap_t, point, before, after,
     hid, raw, raw_hid, send_p, recv_p, cen, gmid, gc, recv_g, mid, gh, slp, inv, out, ing,
     gain_in_b, gain_mid_b, acc_in, acc_mid, packed, slots0, slots1, slots2,
     in_sem, act_sem, out_sem, ing_sem, raw_send, raw_recv,
@@ -184,11 +184,11 @@
         return pl.ds(RAW, size - RAW) if isinstance(k, int) and k == 0 else pl.ds(start, size)
 
     gain_in_b[...] = jnp.broadcast_to(small[pl.ds(0, c)].reshape(1, c), (SUB, c))
-    load_first.wait()
-    each_sub(0, lead, norm)
     pl.semaphore_wait(barrier, len(greeted))
     push_raw(0).start()
     push_raw(1).start()
+    load_first.wait()
+    each_sub(0, lead, norm)
     load_tap[0].wait()
     product(0, 0, product_rows(0, 0, lead))
     load_tap[2].wait()
@@ -328,14 +328,20 @@
 
     each_sub(0, rows, slopes)
 
+    def turn(at):
+        for way in range(2):
+            tap_t[way, :, at] = tap[2 * way, at].T
+
+    tiles(c, turn)
+
     def arrive(k, start, size):
         at = pl.ds(start, size)
         push_g(0, k, at).wait_recv()
         gb = (recv_g[0, at].astype(F32) * before[at]).astype(BF16)
-        gh[at] += nt_dot(gb, tap[2])
+        gh[at] += nn_dot(gb, tap_t[1])
         push_g(1, k, at).wait_recv()
         ga = (recv_g[1, at].astype(F32) * after[at]).astype(BF16)
-        gh[at] += nt_dot(ga, tap[0])
+        gh[at] += nn_dot(ga, tap_t[0])
 
     def terms(at, _):
         acc_in[...] += fold(gh[at] * slp[at] * (act[at].astype(F32) * inv[at]))
@@ -438,6 +444,7 @@
             vmem((rows, c), BF16),
             vmem((rows, c), BF16),
             vmem((3, c, f), BF16),
+            vmem((2, f, c), BF16),
             vmem((f, c), BF16),
             vmem((rows, 1), F32),
             vmem((rows, 1), F32),

time: 100 us -> 99.4 us (level)
  Pallas kernels: 98.2 us -> 97.2 us
    pallas_call x1, Pallas kernels: 95.9 us -> 94.9 us  [body(): pl.pallas_call(functools.partial(kernel, n_seq, n_batch, contig_lengths.s...]
where the time goes in v3:
time: 99.4 us; the launch traced here: 99.2 us
  Pallas kernels  97.2 us (98%)
  other arithmetic  1.38 us (1%)
    pallas_call x1, Pallas kernels, body(): pl.pallas_call(functools.partial(kernel, n_seq, n_batch, contig_lengths.s...  94.9 us
    pallas_call x1, Pallas kernels, body(): pl.pallas_call(finish_kernel, name='tail', out_shape=shapes, in_specs=[an...  2.27 us

profile of v3, /device:TPU:1, one launch (start us, length us, event | category | flops | bytes accessed | tf_op | source)
XLA Modules:
  0.0 99.2 jit_solution(13505362934564024090)
XLA Ops:
  0.6 0.7 convert_bitcast_fusion
  1.3 0.7 select_maximum_fusion.small
  2.0 94.9 %block.1 = (bf16[1,512,1536]{2,1,0:T(8,128)(2,1)S(1)}, bf16[1,512,1536]{2,1,0:T(8,128)(2,1)S(1)}, f32[1536]{0:T(1024)S(1)}, f32[768]{0:T(1024)S(1)}) custom-call(f32[2432]{0:T(1024)S(1)} %select_maximum_fusion.small, bf16[1,512,1536]{2,1,0:T(8,128)(2,1)} %act_hbm.1, bf16[1,512,1536]{2,1,0:T(8,128)(2,1)} %ct_hbm.1, bf16[3,1536,768]{2,1,0:T(8,128)(2,1)} %tap_hbm.1, ...), custom_call_target="tpu_custom_call" | custom-call | flops 9663676416 | bytes 16777216 | tf_op jit(solution)/shard_map/block/pallas_call | solution.py:437
  96.9 2.3 %tail.1 = (bf16[1,512,1536]{2,1,0:T(8,128)(2,1)}, bf16[1,512,1536]{2,1,0:T(8,128)(2,1)}, f32[1536]{0:T(1024)}, f32[768]{0:T(1024)}) custom-call(bf16[1,512,1536]{2,1,0:T(8,128)(2,1)S(1)} %get-tuple-element.8.out, bf16[1,512,1536]{2,1,0:T(8,128)(2,1)S(1)} %get-tuple-element.9.ing, f32[1536]{0:T(1024)S(1)} %get-tuple-element.10.gsum_in, ...), custom_call_target="tpu_custom_call" | custom-call | tf_op jit(solution)/shard_map/tail/pallas_call | solution.py:485

commit v4 on v3

--- a/solution.py
+++ b/solution.py
@@ -338,10 +338,9 @@
         at = pl.ds(start, size)
         push_g(0, k, at).wait_recv()
         gb = (recv_g[0, at].astype(F32) * before[at]).astype(BF16)
-        gh[at] += nn_dot(gb, tap_t[1])
         push_g(1, k, at).wait_recv()
         ga = (recv_g[1, at].astype(F32) * after[at]).astype(BF16)
-        gh[at] += nn_dot(ga, tap_t[0])
+        gh[at] += nn_dot(gb, tap_t[1]) + nn_dot(ga, tap_t[0])
 
     def terms(at, _):
         acc_in[...] += fold(gh[at] * slp[at] * (act[at].astype(F32) * inv[at]))
@@ -353,10 +352,13 @@
         s = jnp.mean(dug * nv, axis=-1, keepdims=True)
         ing[at] = (ct[at].astype(F32) + r * (dug - nv * s)).astype(BF16)
 
+    def terms_and_grad(at, row):
+        terms(at, row)
+        input_grad(at, row)
+
     def backward(k, start, size):
         arrive(k, start, size)
-        each_sub(start, size, terms)
-        each_sub(start, size, input_grad)
+        each_sub(start, size, terms_and_grad)
 
     base, size, count = GROUPS[-1]
     chunks = sum(g[2] for g in GROUPS)

time: 99.4 us -> 99.3 us (level)
  no operation moved by 1% of the time
where the time goes in v4:
time: 99.3 us; the launch traced here: 99.1 us
  Pallas kernels  97.1 us (98%)
  other arithmetic  1.38 us (1%)
    pallas_call x1, Pallas kernels, body(): pl.pallas_call(functools.partial(kernel, n_seq, n_batch, contig_lengths.s...  94.8 us
    pallas_call x1, Pallas kernels, body(): pl.pallas_call(finish_kernel, name='tail', out_shape=shapes, in_specs=[an...  2.27 us

profile of v4, /device:TPU:1, one launch (start us, length us, event | category | flops | bytes accessed | tf_op | source)
XLA Modules:
  0.0 99.1 jit_solution(13854893035257628245)
XLA Ops:
  0.6 0.7 convert_bitcast_fusion
  1.3 0.7 select_maximum_fusion.small
  2.0 94.8 %block.1 = (bf16[1,512,1536]{2,1,0:T(8,128)(2,1)S(1)}, bf16[1,512,1536]{2,1,0:T(8,128)(2,1)S(1)}, f32[1536]{0:T(1024)S(1)}, f32[768]{0:T(1024)S(1)}) custom-call(f32[2432]{0:T(1024)S(1)} %select_maximum_fusion.small, bf16[1,512,1536]{2,1,0:T(8,128)(2,1)} %act_hbm.1, bf16[1,512,1536]{2,1,0:T(8,128)(2,1)} %ct_hbm.1, bf16[3,1536,768]{2,1,0:T(8,128)(2,1)} %tap_hbm.1, ...), custom_call_target="tpu_custom_call" | custom-call | flops 9663676416 | bytes 16777216 | tf_op jit(solution)/shard_map/block/pallas_call | solution.py:439
  96.8 2.3 %tail.1 = (bf16[1,512,1536]{2,1,0:T(8,128)(2,1)}, bf16[1,512,1536]{2,1,0:T(8,128)(2,1)}, f32[1536]{0:T(1024)}, f32[768]{0:T(1024)}) custom-call(bf16[1,512,1536]{2,1,0:T(8,128)(2,1)S(1)} %get-tuple-element.8.out, bf16[1,512,1536]{2,1,0:T(8,128)(2,1)S(1)} %get-tuple-element.9.ing, f32[1536]{0:T(1024)S(1)} %get-tuple-element.10.gsum_in, ...), custom_call_target="tpu_custom_call" | custom-call | tf_op jit(solution)/shard_map/tail/pallas_call | solution.py:487
